TPU v7x, 256 devices: a whole 4x4x8 slice. The times are simulated.
256 devices in a mesh: pairs: 128 (over z, x, y_lo, core), emb: 2 (over y_hi).
Axes of the slice: x: 4, y: 4 (y_hi: 2, y_lo: 2; y = y_hi * 2 + y_lo), z: 8, core: 2. Of those that a mesh axis runs over, the one named last changes fastest.
Arguments:
- round_bits: int32 [2], replicated, may hold values from 0 to 6
- image_embed: bfloat16 [65536, 1152], P('pairs', 'emb'), may hold values from -0.46289062 to 0.46289062
- text_embed: bfloat16 [65536, 1152], P('pairs', 'emb'), may hold values from -0.46289062 to 0.46289062
Outputs:
- image_grad: float32 [65536, 1152], P('pairs', 'emb')
- text_grad: float32 [65536, 1152], P('pairs', 'emb')
All inputs are finite; a program needn't handle non-finite values.
Results may differ from a plain program's by a relative error of at most 0.0025.
Values may be sent and summed in bfloat16 or wider, within the bound.
A program may use at most 64 MiB of HBM per device.

v0:
```python
import functools

import jax
import jax.numpy as jnp
from jax import lax
from jax.experimental import pallas as pl
from jax.experimental.pallas import tpu as pltpu
from jax.sharding import PartitionSpec as P

logit_scale = 10.0
logit_bias = -1.0
PAIR_BITS = 7
CHUNKS = 4
LEAD = 2
MESH = pl.DeviceIdType.MESH


def flipped(index, bit):
    return index + (1 - 2 * ((index // bit) % 2)) * bit


def last(left, right):
    return lax.dot_general(
        left, right, (((1,), (1,)), ((), ())), preferred_element_type=jnp.float32
    )


def first(left, right):
    return lax.dot_general(
        left, right, (((0,), (0,)), ((), ())), preferred_element_type=jnp.float32
    )


def kernel(
    bits,
    image_hbm,
    text_hbm,
    image_out,
    text_out,
    image,
    texts,
    partial,
    partial_out,
    partial_in,
    weights,
    extra_out,
    extra_in,
    image_sum,
    text_sum,
    local_sem,
    text_send,
    text_recv,
    part_send,
    part_recv,
    extra_send,
    extra_recv,
    out_sem,
):
    rows = image.shape[1]
    n = rows // CHUNKS
    rounds = len(bits)
    items = (rounds + 1) * CHUNKS
    pair = lax.axis_index("pairs")
    half = lax.axis_index("emb")

    def partner(r):
        if rounds == 1:
            return flipped(pair, bits[0])
        met = [flipped(pair, bit) for bit in bits]
        return met[0] + (met[1] - met[0]) * r

    def place(t, c):
        return pl.ds(pl.multiple_of(t * rows + c * n, n), n)

    def text_copy(r, c):
        return pltpu.make_async_remote_copy(
            src_ref=text_hbm.at[:, place(0, c)],
            dst_ref=texts.at[:, place(r + 1, c)],
            send_sem=text_send.at[r, c],
            recv_sem=text_recv.at[r, c],
            device_id=(partner(r), half),
            device_id_type=MESH,
        )

    def part_copy(t, c):
        return pltpu.make_async_remote_copy(
            src_ref=partial_out.at[place(t, c)],
            dst_ref=partial_in.at[place(t, c)],
            send_sem=part_send.at[t, c],
            recv_sem=part_recv.at[t, c],
            device_id=(pair, 1 - half),
            device_id_type=MESH,
        )

    def extra_copy(r, c):
        return pltpu.make_async_remote_copy(
            src_ref=extra_out.at[:, place(r, c)],
            dst_ref=extra_in.at[:, place(r, c)],
            send_sem=extra_send.at[r, c],
            recv_sem=extra_recv.at[r, c],
            device_id=(partner(r), half),
            device_id_type=MESH,
        )

    def text_out_copy(c):
        return pltpu.make_async_copy(
            text_sum.at[:, place(0, c)], text_out.at[:, place(0, c)], out_sem.at[c]
        )

    def item(i):
        inner = i - LEAD
        met = (inner >= 0) & (inner < rounds * CHUNKS)
        tile = jnp.where(met, 1 + inner % rounds, 0)
        chunk = jnp.where(
            met, inner // rounds, jnp.where(inner < 0, i, i - rounds * CHUNKS)
        )
        return tile, chunk

    own_image = pltpu.make_async_copy(image_hbm, image, local_sem.at[0])
    own_text = pltpu.make_async_copy(text_hbm, texts.at[:, pl.ds(0, rows)], local_sem.at[1])
    own_image.start()
    own_text.start()
    barrier = pltpu.get_barrier_semaphore()
    pl.semaphore_signal(barrier, inc=1, device_id=(pair, 1 - half), device_id_type=MESH)
    for r in range(rounds):
        pl.semaphore_signal(
            barrier, inc=1, device_id=(partner(r), half), device_id_type=MESH
        )
    pl.semaphore_wait(barrier, rounds + 1)
    for c in range(CHUNKS):
        for r in range(rounds):
            text_copy(r, c).start()
    own_image.wait()
    own_text.wait()

    @pl.loop(0, items)
    def _(i):
        t, c = item(i)

        @pl.when(t > 0)
        def _():
            text_copy(t - 1, c).wait_recv()

        where = place(t, c)
        scores = first(texts[:, where], image[...])
        partial[where, :] = scores
        partial_out[where, :] = scores.astype(jnp.bfloat16)
        part_copy(t, c).start()

    @pl.loop(0, items)
    def _(i):
        t, c = item(i)
        part_copy(t, c).wait_recv()
        where = place(t, c)
        scores = partial[where, :] + partial_in[where, :].astype(jnp.float32)
        logits = logit_scale * scores + logit_bias
        text_row = c * n + lax.broadcasted_iota(jnp.int32, scores.shape, 0)
        image_row = lax.broadcasted_iota(jnp.int32, scores.shape, 1)
        same = text_row == image_row + t * (2 * rows)
        labels = jnp.where(same, 1.0, -1.0)
        chunk = -labels * logit_scale * jax.nn.sigmoid(-labels * logits)
        chunk = chunk.astype(jnp.bfloat16)
        if rounds == 1:
            chunk = jnp.where(t > 0, chunk * 2, chunk)
        weights[where, :] = chunk
        grad = last(image[...], chunk)

        @pl.when(t == 0)
        def _():
            text_sum[:, place(0, c)] = grad

        @pl.when(t > 0)
        def _():
            extra_out[:, place(t - 1, c)] = grad.astype(jnp.bfloat16)
            extra_copy(t - 1, c).start()

    @pl.loop(0, rows // 256)
    def _(m):
        block = pl.ds(pl.multiple_of(m * 256, 256), 256)
        image_sum[:, block] = jnp.dot(
            texts[...], weights[:, block], preferred_element_type=jnp.float32
        )

    image_copy = pltpu.make_async_copy(image_sum, image_out, local_sem.at[0])
    image_copy.start()

    @pl.loop(0, CHUNKS)
    def _(c):
        for r in range(rounds):
            extra_copy(r, c).wait_recv()
            text_sum[:, place(0, c)] += extra_in[:, place(r, c)].astype(jnp.float32)
        text_out_copy(c).start()

    @pl.loop(0, CHUNKS)
    def _(c):
        for r in range(rounds):
            text_copy(r, c).wait_send()
            extra_copy(r, c).wait_send()
        for t in range(rounds + 1):
            part_copy(t, c).wait_send()
        text_out_copy(c).wait()

    image_copy.wait()


def meet(bits, collective_id, image, text):
    width, rows = image.shape
    rounds = len(bits)
    tiles = rounds + 1
    out = jax.ShapeDtypeStruct((width, rows), jnp.float32)
    return pl.pallas_call(
        functools.partial(kernel, bits),
        out_shape=(out, out),
        in_specs=[pl.BlockSpec(memory_space=pl.ANY)] * 2,
        out_specs=(pl.BlockSpec(memory_space=pl.ANY),) * 2,
        scratch_shapes=[
            pltpu.VMEM((width, rows), jnp.bfloat16),
            pltpu.VMEM((width, tiles * rows), jnp.bfloat16),
            pltpu.VMEM((tiles * rows, rows), jnp.float32),
            pltpu.VMEM((tiles * rows, rows), jnp.bfloat16),
            pltpu.VMEM((tiles * rows, rows), jnp.bfloat16),
            pltpu.VMEM((tiles * rows, rows), jnp.bfloat16),
            pltpu.VMEM((width, rounds * rows), jnp.bfloat16),
            pltpu.VMEM((width, rounds * rows), jnp.bfloat16),
            pltpu.VMEM((width, rows), jnp.float32),
            pltpu.VMEM((width, rows), jnp.float32),
            pltpu.SemaphoreType.DMA((2,)),
            pltpu.SemaphoreType.DMA((rounds, CHUNKS)),
            pltpu.SemaphoreType.DMA((rounds, CHUNKS)),
            pltpu.SemaphoreType.DMA((tiles, CHUNKS)),
            pltpu.SemaphoreType.DMA((tiles, CHUNKS)),
            pltpu.SemaphoreType.DMA((rounds, CHUNKS)),
            pltpu.SemaphoreType.DMA((rounds, CHUNKS)),
            pltpu.SemaphoreType.DMA((CHUNKS,)),
        ],
        compiler_params=pltpu.CompilerParams(
            collective_id=collective_id,
            has_side_effects=True,
            vmem_limit_bytes=40 << 20,
        ),
        cost_estimate=pl.CostEstimate(
            flops=2 * (3 * tiles) * rows * rows * width,
            bytes_accessed=12 * rows * width,
            transcendentals=tiles * rows * rows,
        ),
    )(image, text)


def shards(round_bits, image_embed, text_embed):
    low = jnp.minimum(round_bits[0], round_bits[1])
    high = jnp.maximum(round_bits[0], round_bits[1])
    branches = []
    for a in range(PAIR_BITS):
        for b in range(a, PAIR_BITS):
            bits = (1 << a,) if a == b else (1 << a, 1 << b)
            branches.append(functools.partial(meet, bits, len(branches) + 1))
    which = low * PAIR_BITS - low * (low - 1) // 2 + (high - low)
    image_grad, text_grad = lax.switch(which, branches, image_embed.T, text_embed.T)
    return image_grad.T, text_grad.T


def solution(mesh):
    placed = (P(), P("pairs", "emb"), P("pairs", "emb"))
    return jax.shard_map(
        shards,
        mesh=mesh,
        in_specs=placed,
        out_specs=(P("pairs", "emb"), P("pairs", "emb")),
        check_vma=False,
    )
```

profile of v0, /device:TPU:2, one launch (start us, length us, event | category | flops | bytes accessed | tf_op | source)
XLA Modules:
  0.0 73.1 jit_solution(14054309982220956122)
XLA Ops:
  0.6 1.3 %fusion = (s32[1]{0:T(128)}, s32[1]{0:T(128)}) fusion(s32[2]{0:T(128)} %param.31), kind=kLoop, calls=%fused_computation | loop fusion | bytes 16 | tf_op jit(solution)/shard_map/slice | solution.py:250
  4.6 66.5 %conditional.1 = ((f32[576,512]{1,0:T(8,128)S(1)}, f32[576,512]{1,0:T(8,128)S(1)})) conditional(s32[]{:T(128)} %clamp.3, (bf16[576,512]{1,0:T(8,128)(2,1)}, bf16[576,512]{1,0:T(8,128)(2,1)}) %tuple.194, (bf16[576,512]{1,0:T(8,128)(2,1)}, bf16[576,512]{1,0:T(8,128)(2,1)}) %tuple.208, (bf16[576,512]{1,0:T(8,128)(2,1)}, ...), branch_computations={%region_0.1_spmd, %region_1.2_spmd, %region_2.3_spmd, %region_3.4_... | conditional | flops 2717908992 | bytes 3538952 | solution.py:258
  12.3 58.6 %branch_16_fun.1 = (f32[576,512]{1,0:T(8,128)S(1)}, f32[576,512]{1,0:T(8,128)S(1)}) custom-call(bf16[576,512]{1,0:T(8,128)(2,1)} %get-tuple-element.144.image_hbm, bf16[576,512]{1,0:T(8,128)(2,1)} %get-tuple-element.145.text_hbm), custom_call_target="tpu_custom_call" | custom-call | flops 2717908992 | bytes 3538944 | tf_op jit(solution)/shard_map/cond/branch_16_fun/pallas_call | solution.py:211
  71.1 1.0 %copy.63 = f32[512,576]{0,1:T(8,128)} copy(f32[512,576]{0,1:T(8,128)S(1)} %bitcast.6) | data formatting | bytes 2359296
  72.1 1.0 %copy.64 = f32[512,576]{0,1:T(8,128)} copy(f32[512,576]{0,1:T(8,128)S(1)} %bitcast.7) | data formatting | bytes 2359296
where the time goes:
time: 73.3 us; the launch traced here: 73.1 us
  Pallas kernels  58.6 us (80%)
  loops' own time  7.97 us (11%)
  local copies, waits for them, and re-layouts  3.34 us (5%)
  between operations  3.26 us (4%)
    pallas_call x1, Pallas kernels, meet(): pl.pallas_call(functools.partial(kernel, bits), out_shape=(out, out), in_...  58.6 us
    another operation x1, loops' own time, shards(): lax.switch(which, branches, image_embed.T, text_embed.T)  7.97 us
    unnamed x2, local copies, waits for them, and re-layouts  2.03 us

commit v1 on v0

v1 whole, which is shorter than its diff:
```python
import functools

import jax
import jax.numpy as jnp
from jax import lax
from jax.experimental import pallas as pl
from jax.experimental.pallas import tpu as pltpu
from jax.sharding import PartitionSpec as P

logit_scale = 10.0
logit_bias = -1.0
PAIR_BITS = 7
CHUNKS = 4
LEAD = 2
CHAINED = ((4, 8), (16, 64), (32, 64))
MESH = pl.DeviceIdType.MESH


def flipped(index, bit):
    return index + (1 - 2 * ((index // bit) % 2)) * bit


def last(left, right):
    return lax.dot_general(
        left, right, (((1,), (1,)), ((), ())), preferred_element_type=jnp.float32
    )


def first(left, right):
    return lax.dot_general(
        left, right, (((0,), (0,)), ((), ())), preferred_element_type=jnp.float32
    )


class Plan:
    def __init__(self, bits):
        self.bits = bits
        self.chain = bits in CHAINED
        self.rounds = len(bits)
        self.tiles = 1 + self.rounds
        lead = CHUNKS if self.chain else LEAD
        head = ([0], 0, lead)
        tail = ([0], lead, CHUNKS - lead)
        met = [(list(range(1, self.tiles)), 0, CHUNKS)]
        self.score_order = [head, *met, tail]
        if self.chain:
            met = [([2], 0, CHUNKS), ([1], 0, CHUNKS)]
        self.weight_order = [head, *met, tail]
        self.early = self.tiles * CHUNKS - (CHUNKS - lead)


def placed_at(order, i):
    start = 0
    tile, chunk = 0, 0
    for tiles, low, count in order:
        if not count:
            continue
        inner = i - start
        here = tiles[0]
        for k in range(1, len(tiles)):
            here = jnp.where(inner % len(tiles) == k, tiles[k], here)
        tile = jnp.where(inner >= 0, here, tile)
        chunk = jnp.where(inner >= 0, low + inner // len(tiles), chunk)
        start += count * len(tiles)
    return tile, chunk


def kernel(
    plan,
    image_hbm,
    text_hbm,
    image_out,
    text_out,
    held,
    partial,
    partial_out,
    partial_in,
    weights,
    extra_out,
    extra_in,
    image_sum,
    text_sum,
    local_sem,
    held_send,
    held_recv,
    part_send,
    part_recv,
    extra_send,
    extra_recv,
    out_sem,
):
    rows = image_sum.shape[1]
    n = rows // CHUNKS
    tall = image_sum.shape[0] // 2
    tiles = plan.tiles
    items = tiles * CHUNKS
    pair = lax.axis_index("pairs")
    half = lax.axis_index("emb")
    met = [flipped(pair, bit) for bit in plan.bits]
    across = flipped(met[0], plan.bits[1]) if plan.chain else None

    def place(t, c):
        return pl.ds(pl.multiple_of(t * rows + c * n, n), n)

    def back_to(t):
        if plan.rounds == 1:
            return met[0]
        return met[0] + ((across if plan.chain else met[1]) - met[0]) * (t - 1)

    def remote(src, dst, sends, recvs, t, c, device):
        return pltpu.make_async_remote_copy(
            src_ref=src,
            dst_ref=dst,
            send_sem=sends.at[t, c],
            recv_sem=recvs.at[t, c],
            device_id=device,
            device_id_type=MESH,
        )

    def held_copy(t, c, source=text_hbm, slot=0):
        return remote(
            source.at[:, place(slot, c)],
            held.at[:, place(t, c)],
            held_send,
            held_recv,
            t,
            c,
            (back_to(t), half),
        )

    def part_copy(t, c):
        return remote(
            partial_out.at[place(t, c)],
            partial_in.at[place(t, c)],
            part_send,
            part_recv,
            t,
            c,
            (pair, 1 - half),
        )

    def extra_copy(t, c):
        return remote(
            extra_out.at[:, place(t - 1, c)],
            extra_in.at[:, place(t - 1, c)],
            extra_send,
            extra_recv,
            t,
            c,
            (back_to(t), half),
        )

    def text_out_copy(c):
        return pltpu.make_async_copy(
            text_sum.at[:, place(0, c)], text_out.at[:, place(0, c)], out_sem.at[c]
        )

    own_text = pltpu.make_async_copy(text_hbm, held.at[:, pl.ds(0, rows)], local_sem.at[0])
    own_image = pltpu.make_async_copy(
        image_hbm, held.at[:, pl.ds(tiles * rows, rows)], local_sem.at[1]
    )
    own_text.start()
    own_image.start()

    peers = [(pair, 1 - half)] + [(block, half) for block in met]
    if plan.chain:
        peers.append((across, half))
    barrier = pltpu.get_barrier_semaphore()
    for peer in peers:
        pl.semaphore_signal(barrier, inc=1, device_id=peer, device_id_type=MESH)
    pl.semaphore_wait(barrier, len(peers))

    adds = plan.rounds - plan.chain

    @pl.loop(0, adds * CHUNKS)
    def _(i):
        held_copy(1 + i % adds, i // adds).start()

    own_text.wait()
    own_image.wait()

    @pl.loop(0, items)
    def _(i):
        t, c = placed_at(plan.score_order, i)

        @pl.when(t > 0)
        def _():
            held_copy(t, c).wait_recv()

        if plan.chain:

            @pl.when(t == 1)
            def _():
                held_copy(2, c, held, 1).start()

        where = place(t, c)
        scores = first(held[:, where], held[:, pl.ds(tiles * rows, rows)])
        partial[where, :] = scores
        partial_out[where, :] = scores.astype(jnp.bfloat16)
        part_copy(t, c).start()

    def weigh(i):
        t, c = placed_at(plan.weight_order, i)
        part_copy(t, c).wait_recv()
        where = place(t, c)
        scores = partial[where, :] + partial_in[where, :].astype(jnp.float32)
        logits = logit_scale * scores + logit_bias
        text_row = c * n + lax.broadcasted_iota(jnp.int32, scores.shape, 0)
        image_row = lax.broadcasted_iota(jnp.int32, scores.shape, 1)
        same = text_row == image_row + t * (2 * rows)
        labels = jnp.where(same, 1.0, -1.0)
        chunk = -labels * logit_scale * jax.nn.sigmoid(-labels * logits)
        if plan.rounds == 1:
            chunk = chunk * jnp.where(t > 0, 2.0, 1.0)
        chunk = chunk.astype(jnp.bfloat16)
        weights[where, :] = chunk
        if plan.chain:

            @pl.when(t == 1)
            def _():
                extra_copy(2, c).wait_recv()

        @pl.loop(0, 2)
        def _(m):
            down = pl.ds(pl.multiple_of(m * tall, tall), tall)
            grad = last(held[down, pl.ds(tiles * rows, rows)], weights[where, :])

            @pl.when(t == 0)
            def _():
                text_sum[down, place(0, c)] = grad

            @pl.when(t > 0)
            def _():
                extra_out[down, place(t - 1, c)] = grad.astype(jnp.bfloat16)

            if plan.chain:

                @pl.when(t == 1)
                def _():
                    extra_out[down, place(0, c)] = (
                        grad + extra_in[down, place(1, c)].astype(jnp.float32)
                    ).astype(jnp.bfloat16)

        @pl.when(t > 0)
        def _():
            extra_copy(t, c).start()

    def add_image(i):
        blocks = 4
        low = jnp.where(i == items, 0, blocks)
        high = jnp.where(i == items, blocks, blocks * tiles)
        if plan.early == items:
            low = 0
            high = jnp.where(i == items, blocks * tiles, 0)

        @pl.loop(low, high)
        def _(m):
            t = m // blocks
            depth = pl.ds(pl.multiple_of(t * rows, rows), rows)
            down = pl.ds(pl.multiple_of(m // 2 % 2 * tall, tall), tall)
            block = pl.ds(pl.multiple_of(m % 2 * 256, 256), 256)
            product = jnp.dot(
                held[down, depth], weights[depth, block], preferred_element_type=jnp.float32
            )
            begins = t == (0 if plan.early == items else 1)
            image_sum[down, block] = product + jnp.where(
                begins, 0.0, image_sum[down, block]
            )

    @pl.loop(0, items + 1)
    def _(i):
        @pl.when((i == plan.early) | (i == items))
        def _():
            add_image(i)

        @pl.when(i < items)
        def _():
            weigh(i)

    image_copy = pltpu.make_async_copy(image_sum, image_out, local_sem.at[0])
    image_copy.start()

    @pl.loop(0, adds * CHUNKS)
    def _(i):
        t, c = 1 + i % adds, i // adds
        extra_copy(t, c).wait_recv()
        text_sum[:, place(0, c)] += extra_in[:, place(t - 1, c)].astype(jnp.float32)

        @pl.when(t == adds)
        def _():
            text_out_copy(c).start()

    @pl.loop(0, items)
    def _(i):
        t, c = i // CHUNKS, i % CHUNKS
        part_copy(t, c).wait_send()

        @pl.when(t > 0)
        def _():
            held_copy(t, c).wait_send()
            extra_copy(t, c).wait_send()

        @pl.when(t == 0)
        def _():
            text_out_copy(c).wait()

    image_copy.wait()


def meet(bits, collective_id, image, text):
    plan = Plan(bits)
    width, rows = image.shape
    tiles = plan.tiles
    out = jax.ShapeDtypeStruct((width, rows), jnp.float32)
    pairs_of = pltpu.SemaphoreType.DMA((tiles, CHUNKS))
    return pl.pallas_call(
        functools.partial(kernel, plan),
        out_shape=(out, out),
        in_specs=[pl.BlockSpec(memory_space=pl.ANY)] * 2,
        out_specs=(pl.BlockSpec(memory_space=pl.ANY),) * 2,
        scratch_shapes=[
            pltpu.VMEM((width, (tiles + 1) * rows), jnp.bfloat16),
            pltpu.VMEM((tiles * rows, rows), jnp.float32),
            pltpu.VMEM((tiles * rows, rows), jnp.bfloat16),
            pltpu.VMEM((tiles * rows, rows), jnp.bfloat16),
            pltpu.VMEM((tiles * rows, rows), jnp.bfloat16),
            pltpu.VMEM((width, plan.rounds * rows), jnp.bfloat16),
            pltpu.VMEM((width, plan.rounds * rows), jnp.bfloat16),
            pltpu.VMEM((width, rows), jnp.float32),
            pltpu.VMEM((width, rows), jnp.float32),
            pltpu.SemaphoreType.DMA((2,)),
            *[pairs_of] * 6,
            pltpu.SemaphoreType.DMA((CHUNKS,)),
        ],
        compiler_params=pltpu.CompilerParams(
            collective_id=collective_id,
            has_side_effects=True,
            vmem_limit_bytes=40 << 20,
        ),
        cost_estimate=pl.CostEstimate(
            flops=2 * (3 * tiles) * rows * rows * width,
            bytes_accessed=12 * rows * width,
            transcendentals=tiles * rows * rows,
        ),
    )(image, text)


def pick(round_bits, which):
    low = jnp.minimum(round_bits[0], round_bits[1])
    high = jnp.maximum(round_bits[0], round_bits[1])
    which[0] = high + 6 * low - ((low * (low - 1)) >> 1)


def deliver(image_from, text_from, image_out, text_out, sem):
    copies = [
        pltpu.make_async_copy(image_from, image_out, sem.at[0]),
        pltpu.make_async_copy(text_from, text_out, sem.at[1]),
    ]
    for copy in copies:
        copy.start()
    for copy in copies:
        copy.wait()


def shards(round_bits, image_embed, text_embed):
    branches = []
    for a in range(PAIR_BITS):
        for b in range(a, PAIR_BITS):
            bits = (1 << a,) if a == b else (1 << a, 1 << b)
            branches.append(functools.partial(meet, bits, len(branches) + 1))
    which = pl.pallas_call(
        pick,
        out_shape=jax.ShapeDtypeStruct((1,), jnp.int32),
        in_specs=[pl.BlockSpec(memory_space=pltpu.SMEM)],
        out_specs=pl.BlockSpec(memory_space=pltpu.SMEM),
    )(round_bits)
    grads = lax.switch(which[0], branches, image_embed.T, text_embed.T)
    image_grad, text_grad = pl.pallas_call(
        deliver,
        out_shape=tuple(jax.ShapeDtypeStruct(g.shape, g.dtype) for g in grads),
        in_specs=[pl.BlockSpec(memory_space=pl.ANY)] * 2,
        out_specs=(pl.BlockSpec(memory_space=pl.ANY),) * 2,
        scratch_shapes=[pltpu.SemaphoreType.DMA((2,))],
    )(*grads)
    return image_grad.T, text_grad.T


def solution(mesh):
    placed = (P(), P("pairs", "emb"), P("pairs", "emb"))
    return jax.shard_map(
        shards,
        mesh=mesh,
        in_specs=placed,
        out_specs=(P("pairs", "emb"), P("pairs", "emb")),
        check_vma=False,
    )
```

time: 73.3 us -> 35.4 us (0.48)
  Pallas kernels: 58.6 us -> 33.5 us
  loops' own time: 7.97 us -> 0.24 us
  local copies, waits for them, and re-layouts: 3.34 us -> 0 us
  between operations: 3.26 us -> 1.45 us
    pallas_call x1 -> x3, Pallas kernels: 58.6 us -> 33.5 us  [the longest x1 30.9 us: meet(): pl.pallas_call(functools.partial(kernel, plan), out_shape=(out, out), in_...]
    another operation x1, loops' own time: 7.97 us -> 0.24 us  [shards(): grads = lax.switch(which[0], branches, image_embed.T, text_embed.T)]
    unnamed x2 -> x0, local copies, waits for them, and re-layouts: 2.03 us -> none
    slice x1 -> x0, local copies, waits for them, and re-layouts: 1.31 us -> none  [shards(): low = jnp.minimum(round_bits[0], round_bits[1])]
where the time goes in v1:
time: 35.4 us; the launch traced here: 35.2 us
  Pallas kernels  33.5 us (95%)
  between operations  1.45 us (4%)
    pallas_call x1, Pallas kernels, meet(): pl.pallas_call(functools.partial(kernel, plan), out_shape=(out, out), in_...  30.9 us
    pallas_call x1, Pallas kernels, shards(): pl.pallas_call(deliver, out_shape=tuple((jax.ShapeDtypeStruct(g.shape, g....  1.42 us
    pallas_call x1, Pallas kernels, shards(): pl.pallas_call(pick, out_shape=jax.ShapeDtypeStruct((1,), jnp.int32), in_...  1.19 us

profile of v1, /device:TPU:2, one launch (start us, length us, event | category | flops | bytes accessed | tf_op | source)
XLA Modules:
  0.0 35.2 jit_solution(12172764674788455106)
XLA Ops:
  0.6 1.2 %shard_map.50 = s32[1]{0:T(128)} custom-call(s32[2]{0:T(128)} %round_bits.1), custom_call_target="tpu_custom_call" | custom-call | tf_op jit(solution)/shard_map/pallas_call | solution.py:371
  2.5 31.2 %conditional.1 = ((f32[576,512]{1,0:T(8,128)S(1)}, f32[576,512]{1,0:T(8,128)S(1)})) conditional(s32[]{:T(128)} %bitcast, (bf16[576,512]{1,0:T(8,128)(2,1)}, bf16[576,512]{1,0:T(8,128)(2,1)}) %tuple.191, (bf16[576,512]{1,0:T(8,128)(2,1)}, bf16[576,512]{1,0:T(8,128)(2,1)}) %tuple.205, (bf16[576,512]{1,0:T(8,128)(2,1)}, ...), branch_computations={%region_0.0_spmd, %region_1.0_spmd, %region_2.0_spmd, %region_3.0_... | conditional | flops 2717908992 | bytes 3538952 | solution.py:377
  2.5 30.9 %branch_0_fun.1 = (f32[576,512]{1,0:T(8,128)S(1)}, f32[576,512]{1,0:T(8,128)S(1)}) custom-call(bf16[576,512]{1,0:T(8,128)(2,1)} %get-tuple-element.112.image_hbm, bf16[576,512]{1,0:T(8,128)(2,1)} %get-tuple-element.113.text_hbm), custom_call_target="tpu_custom_call" | custom-call | flops 1811939328 | bytes 3538944 | tf_op jit(solution)/shard_map/cond/branch_0_fun/pallas_call | solution.py:316
  33.7 1.4 %shard_map.51 = (f32[576,512]{1,0:T(8,128)}, f32[576,512]{1,0:T(8,128)}) custom-call(f32[576,512]{1,0:T(8,128)S(1)} %get-tuple-element.174.image_from, f32[576,512]{1,0:T(8,128)S(1)} %get-tuple-element.175.text_from), custom_call_target="tpu_custom_call" | custom-call | tf_op jit(solution)/shard_map/pallas_call | solution.py:378

commit v2 on v1

--- a/solution.py
+++ b/solution.py
@@ -11,7 +11,6 @@
 logit_bias = -1.0
 PAIR_BITS = 7
 CHUNKS = 4
-LEAD = 2
 CHAINED = ((4, 8), (16, 64), (32, 64))
 MESH = pl.DeviceIdType.MESH
 
@@ -32,45 +31,72 @@
     )
 
 
+SCORE, WEIGH, IMAGE, ADD = range(4)
+
+
+def a(tile, chunk):
+    return SCORE, tile, chunk
+
+
+def b(tile, chunk):
+    return WEIGH, tile, chunk
+
+
+def i(low, high):
+    return IMAGE, low, high
+
+
+def d(tile, chunk):
+    return ADD, tile, chunk
+
+
+ONE = [
+    a(0, 0), a(0, 1), a(1, 0), a(1, 1), b(0, 0), b(0, 1), b(1, 0), a(1, 2),
+    b(1, 1), a(1, 3), a(0, 2), a(0, 3), b(1, 2), b(1, 3), i(1, 1), b(0, 2),
+    d(1, 0), d(1, 1), d(1, 2), b(0, 3), i(0, 0), d(1, 3),
+]
+TWO = [
+    a(0, 0), a(0, 1), a(1, 0), a(2, 0), a(1, 1), a(2, 1), b(0, 0), b(0, 1),
+    b(1, 0), b(2, 0), a(1, 2), a(2, 2), b(1, 1), b(2, 1), a(1, 3), a(2, 3),
+    a(0, 2), a(0, 3), b(1, 2), b(2, 2), b(1, 3), b(2, 3), i(1, 2), b(0, 2),
+    d(1, 0), d(2, 0), d(1, 1), d(2, 1), d(1, 2), d(2, 2), b(0, 3), i(0, 0),
+    d(1, 3), d(2, 3),
+]
+CHAIN = [
+    a(0, 0), a(0, 1), a(0, 2), a(0, 3), a(1, 0), b(0, 0), a(1, 1), b(0, 1),
+    a(2, 0), b(0, 2), a(1, 2), b(0, 3), a(2, 1), b(2, 0), a(1, 3), a(2, 2),
+    b(2, 1), a(2, 3), b(2, 2), b(1, 0), b(2, 3), b(1, 1), b(1, 2), b(1, 3),
+    i(0, 2), d(1, 0), d(1, 1), d(1, 2), d(1, 3),
+]
+
+
 class Plan:
     def __init__(self, bits):
         self.bits = bits
-        self.chain = bits in CHAINED
         self.rounds = len(bits)
         self.tiles = 1 + self.rounds
-        lead = CHUNKS if self.chain else LEAD
-        head = ([0], 0, lead)
-        tail = ([0], lead, CHUNKS - lead)
-        met = [(list(range(1, self.tiles)), 0, CHUNKS)]
-        self.score_order = [head, *met, tail]
-        if self.chain:
-            met = [([2], 0, CHUNKS), ([1], 0, CHUNKS)]
-        self.weight_order = [head, *met, tail]
-        self.early = self.tiles * CHUNKS - (CHUNKS - lead)
-
-
-def placed_at(order, i):
-    start = 0
-    tile, chunk = 0, 0
-    for tiles, low, count in order:
-        if not count:
-            continue
-        inner = i - start
-        here = tiles[0]
-        for k in range(1, len(tiles)):
-            here = jnp.where(inner % len(tiles) == k, tiles[k], here)
-        tile = jnp.where(inner >= 0, here, tile)
-        chunk = jnp.where(inner >= 0, low + inner // len(tiles), chunk)
-        start += count * len(tiles)
-    return tile, chunk
+        self.chain = bits in CHAINED
+        self.steps = CHAIN if self.chain else TWO if self.rounds == 2 else ONE
+        images = [step for step in self.steps if step[0] == IMAGE]
+        self.image_first = images[0][1]
+
+
+def step_at(order, i):
+    codes = [16 * kind + 4 * tile + chunk for kind, tile, chunk in order]
+    word = 0
+    for k in range(0, len(codes), 5):
+        packed = sum(code << (6 * m) for m, code in enumerate(codes[k : k + 5]))
+        word = jnp.where(i // 5 == k // 5, packed, word)
+    code = lax.shift_right_logical(word, 6 * (i % 5)) % 64
+    return code // 16, code // 4 % 4, code % 4
 
 
 def kernel(
     plan,
     image_hbm,
     text_hbm,
-    image_out,
-    text_out,
+    image_sum,
+    text_sum,
     held,
     partial,
     partial_out,
@@ -78,8 +104,6 @@
     weights,
     extra_out,
     extra_in,
-    image_sum,
-    text_sum,
     local_sem,
     held_send,
     held_recv,
@@ -87,12 +111,12 @@
     part_recv,
     extra_send,
     extra_recv,
-    out_sem,
 ):
     rows = image_sum.shape[1]
     n = rows // CHUNKS
     tall = image_sum.shape[0] // 2
     tiles = plan.tiles
+    own = pl.ds(tiles * rows, rows)
     items = tiles * CHUNKS
     pair = lax.axis_index("pairs")
     half = lax.axis_index("emb")
@@ -150,11 +174,6 @@
             (back_to(t), half),
         )
 
-    def text_out_copy(c):
-        return pltpu.make_async_copy(
-            text_sum.at[:, place(0, c)], text_out.at[:, place(0, c)], out_sem.at[c]
-        )
-
     own_text = pltpu.make_async_copy(text_hbm, held.at[:, pl.ds(0, rows)], local_sem.at[0])
     own_image = pltpu.make_async_copy(
         image_hbm, held.at[:, pl.ds(tiles * rows, rows)], local_sem.at[1]
@@ -179,10 +198,7 @@
     own_text.wait()
     own_image.wait()
 
-    @pl.loop(0, items)
-    def _(i):
-        t, c = placed_at(plan.score_order, i)
-
+    def score(t, c):
         @pl.when(t > 0)
         def _():
             held_copy(t, c).wait_recv()
@@ -194,13 +210,12 @@
                 held_copy(2, c, held, 1).start()
 
         where = place(t, c)
-        scores = first(held[:, where], held[:, pl.ds(tiles * rows, rows)])
+        scores = first(held[:, where], held[:, own])
         partial[where, :] = scores
         partial_out[where, :] = scores.astype(jnp.bfloat16)
         part_copy(t, c).start()
 
-    def weigh(i):
-        t, c = placed_at(plan.weight_order, i)
+    def weigh(t, c):
         part_copy(t, c).wait_recv()
         where = place(t, c)
         scores = partial[where, :] + partial_in[where, :].astype(jnp.float32)
@@ -223,7 +238,7 @@
         @pl.loop(0, 2)
         def _(m):
             down = pl.ds(pl.multiple_of(m * tall, tall), tall)
-            grad = last(held[down, pl.ds(tiles * rows, rows)], weights[where, :])
+            grad = last(held[down, own], weights[where, :])
 
             @pl.when(t == 0)
             def _():
@@ -245,50 +260,40 @@
         def _():
             extra_copy(t, c).start()
 
-    def add_image(i):
-        blocks = 4
-        low = jnp.where(i == items, 0, blocks)
-        high = jnp.where(i == items, blocks, blocks * tiles)
-        if plan.early == items:
-            low = 0
-            high = jnp.where(i == items, blocks * tiles, 0)
-
-        @pl.loop(low, high)
+    def add_image(low, high):
+        @pl.loop(low * 4, high * 4 + 4)
         def _(m):
-            t = m // blocks
+            t = m // 4
             depth = pl.ds(pl.multiple_of(t * rows, rows), rows)
             down = pl.ds(pl.multiple_of(m // 2 % 2 * tall, tall), tall)
             block = pl.ds(pl.multiple_of(m % 2 * 256, 256), 256)
             product = jnp.dot(
                 held[down, depth], weights[depth, block], preferred_element_type=jnp.float32
             )
-            begins = t == (0 if plan.early == items else 1)
             image_sum[down, block] = product + jnp.where(
-                begins, 0.0, image_sum[down, block]
+                t == plan.image_first, 0.0, image_sum[down, block]
             )
 
-    @pl.loop(0, items + 1)
+    @pl.loop(0, len(plan.steps))
     def _(i):
-        @pl.when((i == plan.early) | (i == items))
-        def _():
-            add_image(i)
-
-        @pl.when(i < items)
-        def _():
-            weigh(i)
-
-    image_copy = pltpu.make_async_copy(image_sum, image_out, local_sem.at[0])
-    image_copy.start()
-
-    @pl.loop(0, adds * CHUNKS)
-    def _(i):
-        t, c = 1 + i % adds, i // adds
-        extra_copy(t, c).wait_recv()
-        text_sum[:, place(0, c)] += extra_in[:, place(t - 1, c)].astype(jnp.float32)
-
-        @pl.when(t == adds)
-        def _():
-            text_out_copy(c).start()
+        kind, t, c = step_at(plan.steps, i)
+
+        @pl.when(kind == SCORE)
+        def _():
+            score(t, c)
+
+        @pl.when(kind == WEIGH)
+        def _():
+            weigh(t, c)
+
+        @pl.when(kind == IMAGE)
+        def _():
+            add_image(t, c)
+
+        @pl.when(kind == ADD)
+        def _():
+            extra_copy(t, c).wait_recv()
+            text_sum[:, place(0, c)] += extra_in[:, place(t - 1, c)].astype(jnp.float32)
 
     @pl.loop(0, items)
     def _(i):
@@ -299,12 +304,6 @@
         def _():
             held_copy(t, c).wait_send()
             extra_copy(t, c).wait_send()
-
-        @pl.when(t == 0)
-        def _():
-            text_out_copy(c).wait()
-
-    image_copy.wait()
 
 
 def meet(bits, collective_id, image, text):
@@ -317,7 +316,7 @@
         functools.partial(kernel, plan),
         out_shape=(out, out),
         in_specs=[pl.BlockSpec(memory_space=pl.ANY)] * 2,
-        out_specs=(pl.BlockSpec(memory_space=pl.ANY),) * 2,
+        out_specs=(pl.BlockSpec(memory_space=pltpu.VMEM),) * 2,
         scratch_shapes=[
             pltpu.VMEM((width, (tiles + 1) * rows), jnp.bfloat16),
             pltpu.VMEM((tiles * rows, rows), jnp.float32),
@@ -326,11 +325,8 @@
             pltpu.VMEM((tiles * rows, rows), jnp.bfloat16),
             pltpu.VMEM((width, plan.rounds * rows), jnp.bfloat16),
             pltpu.VMEM((width, plan.rounds * rows), jnp.bfloat16),
-            pltpu.VMEM((width, rows), jnp.float32),
-            pltpu.VMEM((width, rows), jnp.float32),
             pltpu.SemaphoreType.DMA((2,)),
             *[pairs_of] * 6,
-            pltpu.SemaphoreType.DMA((CHUNKS,)),
         ],
         compiler_params=pltpu.CompilerParams(
             collective_id=collective_id,

time: 35.4 us -> 68.4 us (1.93); the launches traced: 35.2 us -> 69 us
  Pallas kernels: 33.5 us -> 67.3 us
    pallas_call x1, Pallas kernels: 30.9 us -> 64.7 us  [meet(): pl.pallas_call(functools.partial(kernel, plan), out_shape=(out, out), in_...]
where the time goes in v2:
time: 68.4 us; the launch traced here: 69 us
  Pallas kernels  67.3 us (98%)
  between operations  1.45 us (2%)
    pallas_call x1, Pallas kernels, meet(): pl.pallas_call(functools.partial(kernel, plan), out_shape=(out, out), in_...  64.7 us
    pallas_call x1, Pallas kernels, shards(): pl.pallas_call(deliver, out_shape=tuple((jax.ShapeDtypeStruct(g.shape, g....  1.42 us

profile of v2, /device:TPU:2, one launch (start us, length us, event | category | flops | bytes accessed | tf_op | source)
XLA Modules:
  0.0 69.0 jit_solution(8314389016637560593)
XLA Ops:
  0.6 1.2 %shard_map.50 = s32[1]{0:T(128)} custom-call(s32[2]{0:T(128)} %round_bits.1), custom_call_target="tpu_custom_call" | custom-call | tf_op jit(solution)/shard_map/pallas_call | solution.py:367
  2.5 64.9 %conditional.1 = ((f32[576,512]{1,0:T(8,128)S(1)}, f32[576,512]{1,0:T(8,128)S(1)})) conditional(s32[]{:T(128)} %bitcast, (bf16[576,512]{1,0:T(8,128)(2,1)}, bf16[576,512]{1,0:T(8,128)(2,1)}) %tuple.191, (bf16[576,512]{1,0:T(8,128)(2,1)}, bf16[576,512]{1,0:T(8,128)(2,1)}) %tuple.205, (bf16[576,512]{1,0:T(8,128)(2,1)}, ...), branch_computations={%region_0.0_spmd, %region_1.0_spmd, %region_2.0_spmd, %region_3.0_... | conditional | flops 2717908992 | bytes 3538952 | solution.py:373
  2.5 64.7 %branch_10_fun.1 = (f32[576,512]{1,0:T(8,128)S(1)}, f32[576,512]{1,0:T(8,128)S(1)}) custom-call(bf16[576,512]{1,0:T(8,128)(2,1)} %get-tuple-element.132.image_hbm, bf16[576,512]{1,0:T(8,128)(2,1)} %get-tuple-element.133.text_hbm), custom_call_target="tpu_custom_call" | custom-call | flops 2717908992 | bytes 3538944 | tf_op jit(solution)/shard_map/cond/branch_10_fun/pallas_call | solution.py:315
  67.4 1.4 %shard_map.51 = (f32[576,512]{1,0:T(8,128)}, f32[576,512]{1,0:T(8,128)}) custom-call(f32[576,512]{1,0:T(8,128)S(1)} %get-tuple-element.174.image_from, f32[576,512]{1,0:T(8,128)S(1)} %get-tuple-element.175.text_from), custom_call_target="tpu_custom_call" | custom-call | tf_op jit(solution)/shard_map/pallas_call | solution.py:374

commit v3 on v2

--- a/solution.py
+++ b/solution.py
@@ -63,10 +63,10 @@
     d(1, 3), d(2, 3),
 ]
 CHAIN = [
-    a(0, 0), a(0, 1), a(0, 2), a(0, 3), a(1, 0), b(0, 0), a(1, 1), b(0, 1),
-    a(2, 0), b(0, 2), a(1, 2), b(0, 3), a(2, 1), b(2, 0), a(1, 3), a(2, 2),
-    b(2, 1), a(2, 3), b(2, 2), b(1, 0), b(2, 3), b(1, 1), b(1, 2), b(1, 3),
-    i(0, 2), d(1, 0), d(1, 1), d(1, 2), d(1, 3),
+    a(0, 0), a(1, 0), b(0, 0), a(1, 1), a(2, 0), a(1, 2), a(2, 1), b(2, 0),
+    a(1, 3), a(2, 2), b(2, 1), a(2, 3), a(0, 1), a(0, 2), a(0, 3), b(2, 2),
+    b(1, 0), b(2, 3), b(1, 1), b(1, 2), b(1, 3), i(1, 2), b(0, 1), b(0, 2),
+    b(0, 3), i(0, 0), d(1, 0), d(1, 1), d(1, 2), d(1, 3),
 ]
 
 
@@ -78,6 +78,7 @@
         self.chain = bits in CHAINED
         self.steps = CHAIN if self.chain else TWO if self.rounds == 2 else ONE
         images = [step for step in self.steps if step[0] == IMAGE]
+        self.ahead = 2
         self.image_first = images[0][1]
 
 
@@ -191,7 +192,7 @@
 
     adds = plan.rounds - plan.chain
 
-    @pl.loop(0, adds * CHUNKS)
+    @pl.loop(0, adds * plan.ahead)
     def _(i):
         held_copy(1 + i % adds, i // adds).start()
 
@@ -202,6 +203,10 @@
         @pl.when(t > 0)
         def _():
             held_copy(t, c).wait_recv()
+
+        @pl.when((t > 0) & (t <= adds) & (c + plan.ahead < CHUNKS))
+        def _():
+            held_copy(t, c + plan.ahead).start()
 
         if plan.chain:
 

time: 68.4 us -> 68.6 us (level)
  no operation moved by 1% of the time
where the time goes in v3:
time: 68.6 us; the launch traced here: 69 us
  Pallas kernels  67.3 us (98%)
  between operations  1.45 us (2%)
    pallas_call x1, Pallas kernels, meet(): pl.pallas_call(functools.partial(kernel, plan), out_shape=(out, out), in_...  64.7 us
    pallas_call x1, Pallas kernels, shards(): pl.pallas_call(deliver, out_shape=tuple((jax.ShapeDtypeStruct(g.shape, g....  1.42 us

profile of v3, /device:TPU:2, one launch (start us, length us, event | category | flops | bytes accessed | tf_op | source)
XLA Modules:
  0.0 69.0 jit_solution(13134373728245924955)
XLA Ops:
  0.6 1.2 %shard_map.50 = s32[1]{0:T(128)} custom-call(s32[2]{0:T(128)} %round_bits.1), custom_call_target="tpu_custom_call" | custom-call | tf_op jit(solution)/shard_map/pallas_call | solution.py:372
  2.5 64.9 %conditional.1 = ((f32[576,512]{1,0:T(8,128)S(1)}, f32[576,512]{1,0:T(8,128)S(1)})) conditional(s32[]{:T(128)} %bitcast, (bf16[576,512]{1,0:T(8,128)(2,1)}, bf16[576,512]{1,0:T(8,128)(2,1)}) %tuple.191, (bf16[576,512]{1,0:T(8,128)(2,1)}, bf16[576,512]{1,0:T(8,128)(2,1)}) %tuple.205, (bf16[576,512]{1,0:T(8,128)(2,1)}, ...), branch_computations={%region_0.0_spmd, %region_1.0_spmd, %region_2.0_spmd, %region_3.0_... | conditional | flops 2717908992 | bytes 3538952 | solution.py:378
  2.5 64.7 %branch_9_fun.1 = (f32[576,512]{1,0:T(8,128)S(1)}, f32[576,512]{1,0:T(8,128)S(1)}) custom-call(bf16[576,512]{1,0:T(8,128)(2,1)} %get-tuple-element.130.image_hbm, bf16[576,512]{1,0:T(8,128)(2,1)} %get-tuple-element.131.text_hbm), custom_call_target="tpu_custom_call" | custom-call | flops 2717908992 | bytes 3538944 | tf_op jit(solution)/shard_map/cond/branch_9_fun/pallas_call | solution.py:320
  67.4 1.4 %shard_map.51 = (f32[576,512]{1,0:T(8,128)}, f32[576,512]{1,0:T(8,128)}) custom-call(f32[576,512]{1,0:T(8,128)S(1)} %get-tuple-element.174.image_from, f32[576,512]{1,0:T(8,128)S(1)} %get-tuple-element.175.text_from), custom_call_target="tpu_custom_call" | custom-call | tf_op jit(solution)/shard_map/pallas_call | solution.py:379
